TPU v7x, 256 devices: a whole 4x4x8 slice. The times are simulated.
256 devices in a mesh: batch: 8 (over x, core), queue: 32 (over y, z).
Axes of the slice: x: 4, y: 4, z: 8, core: 2. Of those that a mesh axis runs over, the one named last changes fastest.
Arguments:
- queries: bfloat16 [8192, 768], P(('batch', 'queue')), may hold values from -6 to 6
- positives: int32 [8192], P(('batch', 'queue')), may hold values from 0 to 131071
- queue: bfloat16 [131072, 768], P('queue'), may hold values from -6 to 6
- pointer: int32 [1], replicated, may hold values from 0 to 131071
- pooled: bfloat16 [4096, 768], P(('batch', 'queue')), may hold values from -6 to 6
- query_projection_weight: float32 [768, 768], P('queue'), may hold values from -0.21875 to 0.21875
- key_weight: float32 [768, 768], P('queue'), may hold values from -0.21875 to 0.21875
Outputs:
- loss: float32 [8192], P(('batch', 'queue'))
- query_grad: float32 [8192, 768], P(('batch', 'queue'))
- new_queue: bfloat16 [131072, 768], P('queue')
- refreshed_key_weight: float32 [768, 768], P('queue')
All inputs are finite; a program needn't handle non-finite values.
Results may differ from a plain program's by a relative error of at most 0.0016.
Values may be sent and summed in bfloat16 or wider, within the bound.
A program may use at most 128 MiB of HBM per device.

v0:
```python
import math

import jax
import jax.numpy as jnp
from jax import lax
from jax.sharding import PartitionSpec as P

sharpness_divisor = 0.05
momentum_rate = 0.9


def local(queries, positives, queue, pointer, pooled, query_projection_weight, key_weight):
    vector_length = queue.shape[1]
    partition_rows = queue.shape[0]
    own_rows = queries.shape[0]
    similarity_multiplier = 1.0 / (sharpness_divisor * math.sqrt(vector_length))
    rows_all, pos_all = (
        lax.all_gather(queries, "queue", axis=0, tiled=True),
        lax.all_gather(positives, "queue", axis=0, tiled=True),
    )
    first_row = lax.axis_index("queue") * partition_rows
    scores = jnp.dot(rows_all, queue.T, preferred_element_type=jnp.float32) * similarity_multiplier
    local_pos = pos_all - first_row
    inside = (local_pos >= 0) & (local_pos < partition_rows)
    bounded_value = jnp.clip(local_pos, 0, partition_rows - 1)
    pos_score = jnp.where(
        inside, jnp.take_along_axis(scores, bounded_value[:, None], axis=1)[:, 0], 0.0
    )
    local_top = jnp.max(scores, axis=1)
    top = lax.pmax(local_top, "queue")
    local_sum = jnp.sum(jnp.exp(scores - top[:, None]), axis=1)
    total, positive = lax.psum((local_sum, pos_score), "queue")
    loss_all = jnp.log(total) + top - positive
    probs = (jnp.exp(scores - top[:, None]) / total[:, None]).astype(jnp.bfloat16)
    positive_key_rows = jnp.where(
        inside[:, None], jnp.take(queue, bounded_value, axis=0).astype(jnp.float32), 0.0
    )
    own_start = lax.axis_index("queue") * own_rows
    grad_whole = lax.psum(
        jnp.dot(probs, queue, preferred_element_type=jnp.float32) - positive_key_rows, "queue"
    )
    grad_sum = lax.dynamic_slice_in_dim(grad_whole, own_start, own_rows, 0)
    query_grad = grad_sum * similarity_multiplier
    loss = lax.dynamic_slice_in_dim(loss_all, own_start, own_rows, 0)
    refreshed_key_weight = (
        momentum_rate * key_weight + (1.0 - momentum_rate) * query_projection_weight
    )
    weight_low = refreshed_key_weight.astype(jnp.bfloat16)
    keys = jnp.dot(
        pooled,
        lax.all_gather(weight_low, "queue", axis=0, tiled=True),
        preferred_element_type=jnp.float32,
    ).astype(jnp.bfloat16)
    incoming_total = keys.shape[0] * lax.axis_size("batch") * lax.axis_size("queue")
    queue_len = partition_rows * lax.axis_size("queue")
    global_rows = first_row + jnp.arange(partition_rows, dtype=jnp.int32)
    offset = (global_rows - pointer[0]) % queue_len
    landing = offset < incoming_total
    every_key = lax.all_gather(keys, ("batch", "queue"), axis=0, tiled=True)
    picked = jnp.take(every_key, jnp.minimum(offset, incoming_total - 1), axis=0)
    new_queue = jnp.where(landing[:, None], picked, queue)
    return (loss, query_grad, new_queue, refreshed_key_weight)


def solution(mesh):
    return jax.shard_map(
        local,
        mesh=mesh,
        in_specs=(
            P(("batch", "queue"), None),
            P(("batch", "queue")),
            P("queue", None),
            P(),
            P(("batch", "queue"), None),
            P("queue", None),
            P("queue", None),
        ),
        out_specs=(
            P(("batch", "queue")),
            P(("batch", "queue"), None),
            P("queue", None),
            P("queue", None),
        ),
        check_vma=False,
    )
```

profile of v0, /device:TPU:47, one launch (start us, length us, event | category | flops | bytes accessed | tf_op | source)
XLA Modules:
  0.0 593.0 jit_solution(7019990946082000886)
XLA Ops:
  7.2 0.0 copy-start
  7.2 0.0 all-gather.4.cloned.1.call-start
  7.2 0.7 all-gather.4.cloned.1.call-update
  7.9 0.0 all-gather.6.cloned.1.call-start
  8.0 1.6 fusion.10
  9.5 0.0 all-gather.6.cloned.1.call-update
  9.6 0.0 all-reduce.4.cloned.1.call-start
  9.6 1.3 dynamic-slice
  11.5 0.9 dynamic-update-slice
  12.4 17.1 %all-reduce = s32[1024]{0:T(1024)S(1)} all-reduce(s32[1024]{0:T(1024)S(1)} %dynamic-update-slice), channel_id=1, replica_groups=mesh['batch'=8,'queue'=32] {'queue'}, use_global_device_ids=true, to_apply=%add | all-reduce | flops 1024 | bytes 8192
  29.6 8.1 %gather_fusion = bf16[1024,768]{1,0:T(8,128)(2,1)S(1)} fusion(bf16[4096,768]{1,0:T(8,128)(2,1)} %param.9, s32[1024]{0:T(1024)S(1)} %get-tuple-element.8), kind=kCustom, calls=%fused_computation | custom fusion | bytes 3149824 | tf_op jit(solution)/shard_map/jit(_take)/gather | solution.py:36
  37.7 46.9 %all-gather.4.cloned.1.call-done = bf16[1024,768]{1,0:T(8,128)(2,1)} async-done(((bf16[32,768]{1,0:T(8,128)(2,1)}), bf16[1024,768]{1,0:T(8,128)(2,1)}) %all-gather.4.cloned.1.call-update) | async-done | bytes 1572880 | tf_op jit(solution)/shard_map/all_gather | solution.py:18
  84.6 12.6 %fusion.11 = (f32[1024]{0:T(1024)S(1)}, f32[1024,4096]{1,0:T(8,128)}) fusion(bf16[1024,768]{1,0:T(8,128)(2,1)} %all-gather.4.cloned.1.call-done, bf16[4096,768]{1,0:T(8,128)(2,1)} %param.9), kind=kOutput, calls=%fused_computation.41 | convolution fusion | flops 6450838528 | bytes 24645632 | tf_op jit(solution)/shard_map/dot_general | solution.py:22
  97.2 15.8 %gather_fusion.2 = f32[1024]{0:T(1024)S(1)} fusion(f32[1024,4096]{1,0:T(8,128)} %get-tuple-element.14, s32[1024]{0:T(1024)S(1)} %bitcast.16), kind=kCustom, calls=%fused_computation.2 | custom fusion | bytes 16384 | tf_op jit(solution)/shard_map/jit(take_along_axis)/gather | solution.py:27
  113.0 49.4 %pmax.7 = f32[1024]{0:T(1024)S(1)} all-reduce(f32[1024]{0:T(1024)S(1)} %get-tuple-element.13), channel_id=1, replica_groups=mesh['batch'=8,'queue'=32] {'queue'}, use_global_device_ids=true, to_apply=%region_1.2 | all-reduce | flops 1024 | bytes 8192 | tf_op jit(solution)/shard_map/pmax | solution.py:30
  162.4 8.1 %fusion = f32[1024]{0:T(1024)S(1)} fusion(f32[1024,4096]{1,0:T(8,128)} %get-tuple-element.14, f32[1024]{0:T(1024)S(1)} %pmax.7), kind=kLoop, calls=%fused_computation.5 | loop fusion | flops 8387584 | bytes 16785408 | tf_op jit(solution)/shard_map/reduce_sum | solution.py:31
  170.5 56.7 %all-reduce.1 = (f32[1024]{0:T(1024)S(1)}, f32[1024]{0:T(1024)S(1)}) all-reduce(f32[1024]{0:T(1024)S(1)} %get-tuple-element.10, f32[1024]{0:T(1024)S(1)} %fusion), channel_id=1, replica_groups=mesh['batch'=8,'queue'=32] {'queue'}, use_global_device_ids=true, to_apply=%region_4.5 | all-reduce | flops 2048 | bytes 16384 | tf_op jit(solution)/shard_map/psum | solution.py:32
  227.2 14.1 %select_subtract_fusion = f32[1024,768]{1,0:T(8,128)} fusion(bf16[4096,768]{1,0:T(8,128)(2,1)} %param.9, f32[1024,4096]{1,0:T(8,128)} %get-tuple-element.14, f32[1024]{0:T(1024)S(1)} %get-tuple-element.5, f32[1024]{0:T(1024)S(1)} %pmax.7, bf16[1024,768]{1,0:T(8,128)(2,1)S(1)} %gather_fusion, pred[1024]{0:T(1024)(128)(4,1)S(1)} %get-tuple-element.11, ...), kind=kOutput, calls=%fused_computation.9 | convolution fusion | flops 6458179584 | bytes 27797504 | tf_op jit(solution)/shard_map/dot_general | solution.py:40
  241.3 0.0 all-reduce.4.cloned.1.call-update
  241.3 0.2 all-gather.8.cloned.1.call-start
  241.6 0.0 all-gather.6.cloned.1.call-done
  241.6 0.0 copy-done
  241.6 2.2 fusion.2
  243.7 0.0 all-gather.8.cloned.1.call-update
  244.5 0.1 compare_select_fusion
  244.6 0.6 dynamic_slice.6
  245.2 187.9 %all-reduce.4.cloned.1.call-done = f32[1024,768]{1,0:T(8,128)} async-done(((f32[1024,768]{1,0:T(8,128)}), f32[1024,768]{1,0:T(8,128)}) %all-reduce.4.cloned.1.call-update) | async-done | bytes 3145744 | tf_op jit(solution)/shard_map/psum | solution.py:39
  433.1 1.5 dynamic-slice_multiply_fusion
  434.6 120.0 %all-gather.8.cloned.1.call-done = bf16[4096,768]{1,0:T(8,128)(2,1)} async-done(((bf16[16,768]{1,0:T(8,128)(2,1)}), bf16[4096,768]{1,0:T(8,128)(2,1)}) %all-gather.8.cloned.1.call-update) | async-done | bytes 6291472 | tf_op jit(solution)/shard_map/all_gather | solution.py:59
  554.6 22.6 %gather_fusion.1 = bf16[4096,768]{1,0:T(8,128)(2,1)} fusion(bf16[4096,768]{1,0:T(8,128)(2,1)} %all-gather.8.cloned.1.call-done, s32[4096]{0:T(1024)S(1)} %broadcast_clamp_fusion), kind=kCustom, calls=%fused_computation.1 | custom fusion | bytes 12599296 | tf_op jit(solution)/shard_map/jit(_take)/gather | solution.py:60
  577.2 9.2 %select_select_fusion = bf16[4096,768]{1,0:T(8,128)(2,1)} fusion(bf16[4096,768]{1,0:T(8,128)(2,1)} %param.9, bf16[4096,768]{1,0:T(8,128)(2,1)} %gather_fusion.1, pred[4096]{0:T(1024)(128)(4,1)S(1)} %get-tuple-element.15, pred[4096]{0:T(1024)(128)(4,1)S(1)} %get-tuple-element.16), kind=kLoop, calls=%fused_computation.8 | loop fusion | flops 6291456 | bytes 18882560 | tf_op jit(solution)/shard_map/jit(_where)/select_n | solution.py:61
  (9 shorter events, 0.1 us)
Async XLA Ops:
  7.2 234.4 %copy-start = (bf16[16,768]{1,0:T(8,128)(2,1)S(1)}, bf16[16,768]{1,0:T(8,128)(2,1)}, u32[]{:S(2)}) copy-start(bf16[16,768]{1,0:T(8,128)(2,1)} %param.11) | copy-start | bytes 73732
  7.2 77.4 %all-gather.4.cloned.1.call-start = ((), (), s32[]{:S(2)}) async-start(), calls=%async_computation | async-start | bytes 1622016 | tf_op jit(solution)/shard_map/all_gather | solution.py:18
  7.9 233.7 %all-gather.6.cloned.1.call-start = ((), (), s32[]{:S(2)}) async-start(), calls=%async_computation.2 | async-start | bytes 1216512 | tf_op jit(solution)/shard_map/all_gather | solution.py:51
  9.6 423.5 %all-reduce.4.cloned.1.call-start = ((), (), s32[]{:S(2)}) async-start(), calls=%async_computation.1 | async-start | bytes 6291456 | tf_op jit(solution)/shard_map/psum | solution.py:39
  241.3 313.3 %all-gather.8.cloned.1.call-start = ((), (), s32[]{:S(2)}) async-start(), calls=%async_computation.3 | async-start | bytes 6316032 | tf_op jit(solution)/shard_map/all_gather | solution.py:59
Sparse Core Ops, SparseCore 0:
  10.6 73.9 all-gather.3
  87.7 73.7 all-gather.5
  241.4 191.5 all-reduce.3
  437.4 117.1 all-gather.7
where the time goes:
time: 597 us; the launch traced here: 593 us
  waiting for transfers between devices  356 us (60%)
  blocking collectives  123 us (21%)
  local copies, waits for them, and re-layouts  49.3 us (8%)
  matrix products  28.9 us (5%)
  other arithmetic  20.6 us (3%)
  between operations  15.2 us (3%)
    psum x1, waiting for transfers between devices, local(): lax.psum(jnp.dot(probs, queue, preferred_element_type=jnp.float32) - posi...  188 us
    all_gather x1, waiting for transfers between devices, local(): every_key = lax.all_gather(keys, ('batch', 'queue'), axis=0, tiled=True)  120 us
    psum x1, blocking collectives, local(): total, positive = lax.psum((local_sum, pos_score), 'queue')  56.7 us
    pmax x1, blocking collectives, local(): top = lax.pmax(local_top, 'queue')  49.4 us
    all_gather x1, waiting for transfers between devices, local(): lax.all_gather(queries, 'queue', axis=0, tiled=True)  46.9 us
    gather x1, local copies, waits for them, and re-layouts, local(): jnp.take(every_key, jnp.minimum(offset, incoming_total - 1), axis=0)  22.6 us
    unnamed x1, blocking collectives  17.1 us
    gather x1, local copies, waits for them, and re-layouts, local(): jnp.take_along_axis(scores, bounded_value[:, None], axis=1)[:, 0]  15.8 us
  transfers between devices with their start and end apart: 4, of which 3 were waited for; matrix products, arithmetic and copies ran while one was open for 11% of the time, Pallas kernels for 0%

commit v1 on v0

v1 whole, which is shorter than its diff:
```python
import functools
import math

import jax
import jax.numpy as jnp
from jax import lax
from jax.experimental import pallas as pl
from jax.experimental.pallas import tpu as pltpu
from jax.sharding import PartitionSpec as P

F32 = jnp.float32
BF16 = jnp.bfloat16
MESH = pl.DeviceIdType.MESH
NY, NZ = 4, 8
D = 768
HALF = D // 2
KEYS = 4096
ROWS = 256
TILE = 512
SIM = 1.0 / (0.05 * math.sqrt(768))
EXP2 = SIM * math.log2(math.e)
RATE = 0.9


def main_kernel(
    q_in, pool_in, pos_in, wq_in, wk_in, queue,
    loss_o, grad_o, ref_o, nq_o, pool_o, w_o,
    Q, GA, GB, POS, S, ACC, OA, OB, QP, ST, STY, STC, STZ, WC, LC,
    SAR, SAL, RAR, RAL, SBR, SBL, RBR, RBL, TA, YA, TB, SCR, SCL, RCR, RCL,
    ssem, rsem, lsem,
):
    b, k = lax.axis_index("batch"), lax.axis_index("queue")
    y, z = k // NZ, k % NZ
    x, c = b // 2, b % 2
    ids = iter(range(96))

    def zdev(d):
        return (b, y * NZ + (z + d + NZ) % NZ)

    def ydev(d):
        return (b, ((y + d + NY) % NY) * NZ + z)

    def xdev(d):
        return (((x + d + 4) % 4) * 2 + c, k)

    core = (b + 1 - 2 * c, k)

    def rcopy(src, dst, dev):
        i = next(ids)
        return pltpu.make_async_remote_copy(
            src_ref=src, dst_ref=dst, send_sem=ssem.at[i], recv_sem=rsem.at[i],
            device_id=dev, device_id_type=MESH,
        )

    pending = []

    def start(src, dst, dev):
        cp = rcopy(src, dst, dev)
        cp.start()
        pending.append(cp)
        return cp

    load_q = pltpu.make_async_copy(queue, Q, lsem.at[0])
    load_q.start()
    copy_nq = pltpu.make_async_copy(queue, nq_o, lsem.at[1])
    copy_nq.start()

    refreshed = RATE * wk_in[...] + (1.0 - RATE) * wq_in[...]
    ref_o[...] = refreshed
    low = jnp.where(c == 0, refreshed[:, :HALF], refreshed[:, HALF:])
    tail = jnp.concatenate([low[16:24], jnp.zeros((8, HALF), F32)], axis=0)
    GA[y, z, 0:16] = q_in[0:16]
    GA[y, z, 16:32] = pool_in[...]
    GB[y, z, 0:16] = q_in[16:32]
    GB[y, z, 16:32] = jnp.concatenate([low[0:16], tail], axis=1).astype(BF16)
    POS[y, z] = pos_in[...]

    barrier = pltpu.get_barrier_semaphore()
    peers = [zdev(d) for d in range(1, NZ)] + [ydev(d) for d in range(1, NY)]
    peers += [xdev(1), xdev(3), core]
    for dev in peers:
        pl.semaphore_signal(barrier, inc=1, device_id=dev, device_id_type=MESH)
    pl.semaphore_wait(barrier, len(peers))

    pos_y = [start(POS.at[y, z], POS.at[y, z], ydev(d)) for d in (1, 2, 3)]
    a_y = [start(GA.at[y, z], GA.at[y, z], ydev(d)) for d in (1, 3, 2)]

    def zi(d):
        return (z + d + NZ) % NZ

    def yi(d):
        return (y + d + NY) % NY

    def bring(s):
        r, l = zi(1 - s), zi(s - 1)
        if s < 4:
            return (start(GB.at[y, r], GB.at[y, r], zdev(1)),
                    start(GB.at[y, l], GB.at[y, l], zdev(-1)))
        return (start(GB.at[y, r, :, :HALF], GB.at[y, r, :, :HALF], zdev(1)),
                start(GB.at[y, l, :, HALF:], GB.at[y, l, :, HALF:], zdev(-1)))

    def aring(s):
        r, l = zi(1 - s), zi(s - 1)
        if s < 4:
            return (start(GA.at[:, r], GA.at[:, r], zdev(1)),
                    start(GA.at[:, l], GA.at[:, l], zdev(-1)))
        return (start(GA.at[:, r, :, :HALF], GA.at[:, r, :, :HALF], zdev(1)),
                start(GA.at[:, l, :, HALF:], GA.at[:, l, :, HALF:], zdev(-1)))

    def got(pair):
        for cp in pair:
            cp.wait_recv()

    bz = bring(1)
    got(pos_y)
    pos_z = [start(POS.at[:, z], POS.at[:, z], zdev(d)) for d in range(1, NZ)]
    got(a_y)
    az = aring(1)
    got(bz)
    bz = bring(2)
    got(pos_z)
    load_q.wait()

    posf = POS[:, :, 0, :].reshape(NY * NZ, 128).astype(F32)
    post = posf.T - (k * KEYS).astype(F32)

    def positives(p):
        col = jnp.concatenate([post[0:32, 8 * p + j:8 * p + j + 1] for j in range(8)], axis=0)
        for t in range(KEYS // TILE):
            at = lax.broadcasted_iota(jnp.int32, (ROWS, TILE), 1) + t * TILE
            hot = jnp.where(at.astype(F32) == col, 1.0, 0.0).astype(BF16)
            d = jnp.dot(hot, Q[t * TILE:(t + 1) * TILE, :], preferred_element_type=F32)
            if t == 0:
                ACC[...] = d
            else:
                ACC[...] += d
        QP[8 * p:8 * p + 8] = ACC[...].reshape(8, 32, D).astype(BF16)

    positives(0)
    got(bz)
    bz = bring(3)
    got(az)
    az = aring(2)
    positives(1)
    got(bz)
    bz = bring(4)
    got(az)
    az = aring(3)
    positives(2)
    got(bz)
    by = (start(GB.at[y], GB.at[y], ydev(1)), start(GB.at[y], GB.at[y], ydev(-1)))
    got(az)
    az = aring(4)
    positives(3)
    got(by)
    u, d = yi(-1), yi(1)
    by = (start(GB.at[u, :, :, :HALF], GB.at[u, :, :, :HALF], ydev(1)),
          start(GB.at[d, :, :, HALF:], GB.at[d, :, :, HALF:], ydev(-1)))
    got(az)

    mine = GA.at[:, :, 16:32, :]
    own_pool = pltpu.make_async_copy(mine, pool_o.at[b], lsem.at[2])
    own_pool.start()
    px = (start(mine, pool_o.at[b], xdev(1)), start(mine, pool_o.at[b], xdev(-1)))
    cs = [start(mine, pool_o.at[b], core)]
    got(by)
    wmine = GB.at[:, :, 16:32, :]
    own_w = pltpu.make_async_copy(wmine, w_o.at[c], lsem.at[3])
    own_w.start()
    cs.append(start(wmine, w_o.at[c], core))

    lane = lax.broadcasted_iota(jnp.int32, (ROWS, 128), 1)

    def chunk(g, carry):
        X = jnp.concatenate(
            [GA[g, :, 0:16].reshape(128, D), GB[g, :, 0:16].reshape(128, D)], axis=0)
        R = jnp.concatenate(
            [QP[pl.ds(g * 8, 8), 0:16].reshape(128, D), QP[pl.ds(g * 8, 8), 16:32].reshape(128, D)], axis=0)
        ps = jnp.sum(X.astype(F32) * R.astype(F32), axis=1, keepdims=True)
        mx = jnp.full((ROWS, 128), -3e38, F32)
        for t in range(KEYS // TILE):
            s = lax.dot_general(X, Q[t * TILE:(t + 1) * TILE, :], (((1,), (1,)), ((), ())),
                                preferred_element_type=F32)
            S[:, t * TILE:(t + 1) * TILE] = s
            for j in range(TILE // 128):
                mx = jnp.maximum(mx, s[:, j * 128:(j + 1) * 128])
        m = jnp.max(mx, axis=1, keepdims=True)
        total = jnp.zeros((ROWS, 128), F32)
        for t in range(KEYS // TILE):
            e = jnp.exp2((S[:, t * TILE:(t + 1) * TILE] - m) * EXP2)
            for j in range(TILE // 128):
                total = total + e[:, j * 128:(j + 1) * 128]
            d = jnp.dot(e.astype(BF16), Q[t * TILE:(t + 1) * TILE, :], preferred_element_type=F32)
            if t == 0:
                ACC[...] = d
            else:
                ACC[...] += d
        l = jnp.sum(total, axis=1, keepdims=True)
        OA[g] = ACC[0:128].reshape(NZ, 16, D)
        OB[g] = ACC[128:256].reshape(NZ, 16, D)
        cols = jnp.where(lane == 0, m, jnp.where(lane == 1, l, ps))
        ST[:, pl.ds(pl.multiple_of(g * ROWS, ROWS), ROWS)] = cols.T[0:8]
        return carry

    lax.fori_loop(0, 2, chunk, 0)
    got(px)
    left, right = ((x + 3) % 4) * 2 + c, ((x + 1) % 4) * 2 + c
    px = (start(pool_o.at[left, :, :, :, :HALF], pool_o.at[left, :, :, :, :HALF], xdev(1)),
          start(pool_o.at[right, :, :, :, HALF:], pool_o.at[right, :, :, :, HALF:], xdev(-1)))
    cs.append(start(pool_o.at[left], pool_o.at[left], core))
    cs.append(start(pool_o.at[right], pool_o.at[right], core))
    lax.fori_loop(2, 4, chunk, 0)

    def combine(ref, n):
        parts = [ref[i] for i in range(n)]
        top = functools.reduce(jnp.maximum, [p[0:1] for p in parts])
        total = sum(p[1:2] * jnp.exp2((p[0:1] - top) * EXP2) for p in parts)
        positive = sum(p[2:3] for p in parts)
        return top, total, positive

    STY[y] = ST[...]
    sy = [start(ST, STY.at[y], ydev(d)) for d in (1, 2, 3)]
    got(sy)
    top, total, positive = combine(STY, NY)
    STC[...] = jnp.concatenate([top, total, positive, jnp.zeros((5, 1024), F32)], axis=0)
    STZ[z] = STC[...]
    sz = [start(STC, STZ.at[z], zdev(d)) for d in range(1, NZ)]
    got(sz)
    top, total, positive = combine(STZ, NZ)
    w = jnp.exp2((ST[0:1] - top) * EXP2) / total
    loss = jnp.log(total) + (top - positive) * SIM
    LC[...] = jnp.broadcast_to(loss, (128, 1024)).T
    WC[...] = jnp.broadcast_to(w, (128, 1024)).T
    at = pl.multiple_of(y * ROWS + z * 16, 16)
    loss_o[0:16] = LC[pl.ds(at, 16), :]
    loss_o[16:32] = LC[pl.ds(at + 128, 16), :]

    def scale(g, carry):
        base = pl.multiple_of(g * ROWS, ROWS)
        for j in range(D // 128):
            n = slice(j * 128, (j + 1) * 128)
            OA[g, :, :, n] = (OA[g, :, :, n] * WC[pl.ds(base, 128), :].reshape(NZ, 16, 128)
                              - QP[pl.ds(g * 8, 8), 0:16, n].astype(F32))
            OB[g, :, :, n] = (OB[g, :, :, n] * WC[pl.ds(base + 128, 128), :].reshape(NZ, 16, 128)
                              - QP[pl.ds(g * 8, 8), 16:32, n].astype(F32))
        return carry

    lax.fori_loop(0, 4, scale, 0)

    class Ring:
        def __init__(self, n, me, dev, get, sr, sl, rr, rl):
            self.n, self.h, self.me, self.dev, self.get = n, n // 2, me, dev, get
            self.sr, self.sl, self.rr, self.rl = sr, sl, rr, rl
            self.s, self.pair = 0, None

        def step(self):
            n, h = self.n, self.h
            self.s += 1
            s = self.s
            dr, dl = (self.me + h + 1 - s) % n, (self.me + n - h - 1 + s) % n
            sr, sl, rr, rl = (r.at[s - 1] for r in (self.sr, self.sl, self.rr, self.rl))
            if s == 1:
                sr[..., :HALF] = self.get(dr)[..., :HALF]
                sl[..., HALF:] = self.get(dl)[..., HALF:]
                sr, rr = (r.at[..., :HALF] for r in (sr, rr))
                sl, rl = (r.at[..., HALF:] for r in (sl, rl))
            else:
                got(self.pair)
                pr, plf = self.rr.at[s - 2], self.rl.at[s - 2]
                if s == 2:
                    sr[..., :HALF] = self.get(dr)[..., :HALF] + pr[..., :HALF]
                    sr[..., HALF:] = self.get(dr)[..., HALF:]
                    sl[..., :HALF] = self.get(dl)[..., :HALF]
                    sl[..., HALF:] = self.get(dl)[..., HALF:] + plf[..., HALF:]
                else:
                    sr[...] = self.get(dr) + pr[...]
                    sl[...] = self.get(dl) + plf[...]
            self.pair = (start(sr, rr, self.dev(1)), start(sl, rl, self.dev(-1)))

        def end(self):
            got(self.pair)
            return self.get(self.me) + self.rr[self.h - 1] + self.rl[self.h - 1]

    ra = Ring(NZ, z, zdev, lambda d: OA[:, d], SAR, SAL, RAR, RAL)
    rb = Ring(NY, y, ydev, lambda d: OB[d], SBR, SBL, RBR, RBL)
    rc = Ring(NZ, z, zdev, lambda d: TB[d], SCR, SCL, RCR, RCL)
    ra.step()
    rb.step()
    ra.step()
    rb.step()
    ra.step()
    TB[...] = rb.end()
    rc.step()
    ra.step()
    rc.step()
    got(px)
    far = ((x + 2) % 4) * 2 + c
    cs.append(start(pool_o.at[far], pool_o.at[far], core))
    rc.step()
    TA[...] = ra.end()
    YA[y] = TA[y]
    ya = [start(TA.at[yi(d)], YA.at[y], ydev(d)) for d in (1, 2, 3)]
    rc.step()
    grad_o[16:32] = rc.end() * SIM
    got(ya)
    grad_o[0:16] = (YA[0] + YA[1] + YA[2] + YA[3]) * SIM
    got(cs)
    for cp in pending:
        cp.wait_send()
    own_pool.wait()
    own_w.wait()
    copy_nq.wait()


def any_spec():
    return pl.BlockSpec(memory_space=pl.ANY)


def vmem_spec():
    return pl.BlockSpec(memory_space=pltpu.VMEM)


def run_main(queries, pooled, pos, wq, wk, queue):
    n = 96
    z4, y2 = (4, NY, 16, D), (2, NZ, 16, D)
    scratch = [
        pltpu.VMEM((KEYS, D), BF16), pltpu.VMEM((NY, NZ, 32, D), BF16), pltpu.VMEM((NY, NZ, 32, D), BF16),
        pltpu.VMEM((NY, NZ, 8, 128), jnp.int32), pltpu.VMEM((ROWS, KEYS), F32), pltpu.VMEM((ROWS, D), F32),
        pltpu.VMEM((NY, NZ, 16, D), F32), pltpu.VMEM((NY, NZ, 16, D), F32), pltpu.VMEM((32, 32, D), BF16),
        pltpu.VMEM((8, 1024), F32), pltpu.VMEM((NY, 8, 1024), F32), pltpu.VMEM((8, 1024), F32),
        pltpu.VMEM((NZ, 8, 1024), F32), pltpu.VMEM((1024, 128), F32), pltpu.VMEM((1024, 128), F32),
    ]
    scratch += [pltpu.VMEM(z4, F32)] * 4 + [pltpu.VMEM(y2, F32)] * 4
    scratch += [pltpu.VMEM((NY, 16, D), F32)] * 2 + [pltpu.VMEM((NZ, 16, D), F32)]
    scratch += [pltpu.VMEM((4, 16, D), F32)] * 4
    scratch += [pltpu.SemaphoreType.DMA((n,)), pltpu.SemaphoreType.DMA((n,)), pltpu.SemaphoreType.DMA((4,))]
    return pl.pallas_call(
        main_kernel,
        name="retrieval",
        out_shape=[
            jax.ShapeDtypeStruct((32, 128), F32), jax.ShapeDtypeStruct((32, D), F32),
            jax.ShapeDtypeStruct((24, D), F32), jax.ShapeDtypeStruct((KEYS, D), BF16),
            jax.ShapeDtypeStruct((8, NY, NZ, 16, D), BF16), jax.ShapeDtypeStruct((2, NY, NZ, 16, D), BF16),
        ],
        in_specs=[vmem_spec()] * 5 + [any_spec()],
        out_specs=[vmem_spec()] * 3 + [any_spec()] * 3,
        scratch_shapes=scratch,
        compiler_params=pltpu.CompilerParams(
            collective_id=0, has_side_effects=True, vmem_limit_bytes=60 * 2**20),
        cost_estimate=pl.CostEstimate(flops=20 * 10**9, bytes_accessed=32 * 10**6, transcendentals=4 * 10**6),
    )(queries, pooled, pos, wq, wk, queue)


BLK = 256


def enqueue_kernel(shift_ref, pool, w, nq_in, nq, PV, WV, WF, WB, KS, OLD, NEW, sem):
    shift = shift_ref[0]

    @pl.when((shift > -KEYS) & (shift < KEYS))
    def _():
        load_p = pltpu.make_async_copy(pool, PV, sem.at[0])
        load_p.start()
        load_w = pltpu.make_async_copy(w, WV, sem.at[1])
        load_w.start()
        load_w.wait()
        for core in range(2):
            n = slice(core * HALF, (core + 1) * HALF)
            for i in range(32):
                part = WV[core, i].astype(F32)
                WF[24 * i:24 * i + 16, n] = part[:, :HALF]
                WF[24 * i + 16:24 * i + 24, n] = part[0:8, HALF:]
        WB[...] = WF[...].astype(BF16)
        load_p.wait()
        first = jnp.maximum(shift, 0)
        last = jnp.minimum(shift, 0) + KEYS

        def make(i, carry):
            r = pl.multiple_of(i * BLK, BLK)
            keys = jnp.dot(PV[pl.ds(r, BLK), :], WB[...], preferred_element_type=F32)
            KS[pl.ds(r + BLK, BLK), :] = keys.astype(BF16).astype(F32)
            return carry

        lax.fori_loop(first // BLK, (last + BLK - 1) // BLK, make, 0)

        def put(i, carry):
            r = pl.multiple_of(i * BLK, BLK)
            fetch = pltpu.make_async_copy(nq.at[pl.ds(r, BLK), :], OLD, sem.at[2])
            fetch.start()
            fetch.wait()
            at = r + shift
            ok = lax.broadcasted_iota(jnp.int32, (BLK, D), 0) + at
            base = pl.multiple_of((at + BLK) // 8 * 8, 8)
            window = KS[pl.ds(base, BLK + 8), :]
            new = pltpu.roll(window, (BLK + 8) - (at + BLK - base), 0)[:BLK]
            NEW[...] = jnp.where((ok >= 0) & (ok < KEYS), new, OLD[...].astype(F32)).astype(BF16)
            send = pltpu.make_async_copy(NEW, nq.at[pl.ds(r, BLK), :], sem.at[3])
            send.start()
            send.wait()
            return carry

        begin = first - shift
        end = last - shift
        lax.fori_loop(begin // BLK, (end + BLK - 1) // BLK, put, 0)


def run_enqueue(shift, pool, w, nq):
    return pl.pallas_call(
        enqueue_kernel,
        name="enqueue",
        out_shape=jax.ShapeDtypeStruct((KEYS, D), BF16),
        in_specs=[pl.BlockSpec(memory_space=pltpu.SMEM)] + [any_spec()] * 3,
        out_specs=any_spec(),
        scratch_shapes=[
            pltpu.VMEM((KEYS, D), BF16), pltpu.VMEM((2, 32, 16, D), BF16), pltpu.VMEM((D, D), F32),
            pltpu.VMEM((D, D), BF16), pltpu.VMEM((KEYS + 2 * BLK + 8, D), F32), pltpu.VMEM((BLK, D), BF16),
            pltpu.VMEM((BLK, D), BF16), pltpu.SemaphoreType.DMA((4,)),
        ],
        input_output_aliases={3: 0},
        compiler_params=pltpu.CompilerParams(vmem_limit_bytes=60 * 2**20),
    )(shift, pool, w, nq)


def local(queries, positives, queue, pointer, pooled, query_projection_weight, key_weight):
    pos = jnp.broadcast_to(jnp.pad(positives, (0, 96))[None, :], (8, 128))
    loss, grad, refreshed, nq, pool, w = run_main(
        queries, pooled, pos, query_projection_weight, key_weight, queue)
    first_row = lax.axis_index("queue") * KEYS
    shift = (first_row - pointer + KEYS * NY * NZ) % (KEYS * NY * NZ)
    shift = jnp.where(shift >= KEYS, shift - KEYS * NY * NZ, shift)
    new_queue = run_enqueue(shift, pool.reshape(KEYS, D), w.reshape(2, 32, 16, D), nq)
    return loss[:, 0], grad, new_queue, refreshed


def solution(mesh):
    both = P(("batch", "queue"), None)
    one = P("queue", None)
    return jax.shard_map(
        local,
        mesh=mesh,
        in_specs=(both, P(("batch", "queue")), one, P(), both, one, one),
        out_specs=(P(("batch", "queue")), both, one, one),
        check_vma=False,
    )
```

time: 597 us -> 250 us (0.42)
  waiting for transfers between devices: 356 us -> 0 us
  Pallas kernels: 0 us -> 238 us
  blocking collectives: 123 us -> 0 us
  local copies, waits for them, and re-layouts: 49.3 us -> 9.81 us
  matrix products: 28.9 us -> 0 us
  other arithmetic: 20.6 us -> 0 us
  between operations: 15.2 us -> 1.33 us
    pallas_call x0 -> x2, Pallas kernels: none -> 238 us  [the longest x1 195 us: run_main(): pl.pallas_call(main_kernel, name='retrieval', out_shape=[jax.ShapeDtypeSt...]
    psum x1 -> x0, waiting for transfers between devices: 188 us -> none  [local(): lax.psum(jnp.dot(probs, queue, preferred_element_type=jnp.float32) - posi...]
    all_gather x3 -> x0, waiting for transfers between devices: 167 us -> none  [the longest x1 120 us: local(): every_key = lax.all_gather(keys, ('batch', 'queue'), axis=0, tiled=True)]
    psum x1 -> x0, blocking collectives: 56.7 us -> none  [local(): total, positive = lax.psum((local_sum, pos_score), 'queue')]
    pmax x1 -> x0, blocking collectives: 49.4 us -> none  [local(): top = lax.pmax(local_top, 'queue')]
    gather x3 -> x0, local copies, waits for them, and re-layouts: 46.5 us -> none  [the longest x1 22.6 us: local(): jnp.take(every_key, jnp.minimum(offset, incoming_total - 1), axis=0)]
    dot_general x3 -> x0, matrix products: 28.9 us -> none  [the longest x1 14.1 us: local(): jnp.dot(probs, queue, preferred_element_type=jnp.float32)]
    unnamed x1 -> x0, blocking collectives: 17.1 us -> none
  transfers between devices with their start and end apart: 4 -> 0, of which waited for: 3 -> 0; matrix products, arithmetic and copies ran while one was open for 11% -> 0% of each run, Pallas kernels for 0% -> 0%
where the time goes in v1:
time: 250 us; the launch traced here: 249 us
  Pallas kernels  238 us (95%)
  local copies, waits for them, and re-layouts  9.81 us (4%)
    pallas_call x1, Pallas kernels, run_main(): pl.pallas_call(main_kernel, name='retrieval', out_shape=[jax.ShapeDtypeSt...  195 us
    pallas_call x1, Pallas kernels, run_enqueue(): pl.pallas_call(enqueue_kernel, name='enqueue', out_shape=jax.ShapeDtypeSt...  42.6 us
    unnamed x7, local copies, waits for them, and re-layouts  7.21 us

profile of v1, /device:TPU:47, one launch (start us, length us, event | category | flops | bytes accessed | tf_op | source)
XLA Modules:
  0.0 248.8 jit_solution(3668481247106484860)
XLA Ops:
  1.3 0.7 pad.4
  2.0 0.6 broadcast_in_dim.2.pos_in
  2.6 195.1 %retrieval.1 = (f32[32,128]{1,0:T(8,128)}, f32[32,768]{1,0:T(8,128)}, f32[24,768]{1,0:T(8,128)}, bf16[4096,768]{1,0:T(8,128)(2,1)}, bf16[8,4,8,16,768]{4,3,2,1,0...) custom-call(bf16[32,768]{1,0:T(8,128)(2,1)} %q_in.1, bf16[16,768]{1,0:T(8,128)(2,1)} %pool_in.1, ...), custom_call_target="tpu_custom_call" | custom-call | flops 20000000000 | bytes 32000000 | tf_op jit(solution)/shard_map/retrieval/pallas_call | solution.py:337
  197.7 1.3 slice_reduce_fusion
  199.0 0.0 copy-start
  199.0 42.6 %enqueue.1 = bf16[4096,768]{1,0:T(8,128)(2,1)} custom-call(s32[1]{0:T(128)S(6)} %select_n.12.shift_ref, bf16[4096,768]{1,0:T(8,128)(2,1)} %bitcast.3, bf16[2,32,16,768]{3,2,1,0:T(8,128)(2,1)} %bitcast.4, bf16[4096,768]{1,0:T(8,128)(2,1)} %get-tuple-element.14.nq_in), custom_call_target="tpu_custom_call", output_to_operand_aliasing={{}: (3, {})} | custom-call | tf_op jit(solution)/shard_map/enqueue/pallas_call | solution.py:408
  241.6 0.0 copy-done
  241.6 0.6 copy.17
  242.2 0.0 copy-start.1
  242.2 5.9 %copy.18 = bf16[4096,768]{1,0:T(8,128)(2,1)} copy(bf16[4096,768]{1,0:T(8,128)(2,1)} %enqueue.1) | data formatting | bytes 12582912
  248.2 0.0 copy-done.1
  248.2 0.6 copy.19
Async XLA Ops:
  199.0 42.6 %copy-start = (f32[32,768]{1,0:T(8,128)S(1)}, f32[32,768]{1,0:T(8,128)}, u32[]{:S(2)}) copy-start(f32[32,768]{1,0:T(8,128)} %get-tuple-element.21) | copy-start | bytes 294916
  242.2 5.9 %copy-start.1 = (f32[24,768]{1,0:T(8,128)S(1)}, f32[24,768]{1,0:T(8,128)}, u32[]{:S(2)}) copy-start(f32[24,768]{1,0:T(8,128)} %get-tuple-element.23) | copy-start | bytes 221188

commit v2 on v1

v2 whole, which is shorter than its diff:
```python
import functools
import math

import jax
import jax.numpy as jnp
from jax import lax
from jax.experimental import pallas as pl
from jax.experimental.pallas import tpu as pltpu
from jax.sharding import PartitionSpec as P

F32 = jnp.float32
BF16 = jnp.bfloat16
MESH = pl.DeviceIdType.MESH
NY, NZ = 4, 8
D = 768
HALF = D // 2
KEYS = 4096
ROWS = 256
TILE = 512
SIM = 1.0 / (0.05 * math.sqrt(768))
EXP2 = SIM * math.log2(math.e)
RATE = 0.9


def main_kernel(
    q_in, pool_in, pos_in, wq_in, wk_in, queue,
    loss_o, grad_o, ref_o, keys_o,
    Q, GA, GB, GP, GW, POSY, POSC, POSZ, XC, S, ACC, OA, OB, QP, WH, WF, WB, KV, PALL,
    SA, SAY, SAC, SAZ, SB, SBY, SBC, SBZ, LS, WC,
    SAR, SAL, RAR, RAL, SBR, SBL, RBR, RBL, TA, YA, TB, SCR, SCL, RCR, RCL,
    ssem, rsem, lsem,
):
    b, k = lax.axis_index("batch"), lax.axis_index("queue")
    y, z = k // NZ, k % NZ
    x, c = b // 2, b % 2
    ids = iter(range(NSEM))

    def zi(d):
        return (z + d + NZ) % NZ

    def yi(d):
        return (y + d + NY) % NY

    def zdev(d):
        return (b, y * NZ + zi(d))

    def ydev(d):
        return (b, yi(d) * NZ + z)

    def xdev(d):
        return (((x + d + 4) % 4) * 2 + c, k)

    core = (b + 1 - 2 * c, k)
    pending = []

    def start(src, dst, dev):
        i = next(ids)
        cp = pltpu.make_async_remote_copy(
            src_ref=src, dst_ref=dst, send_sem=ssem.at[i], recv_sem=rsem.at[i],
            device_id=dev, device_id_type=MESH,
        )
        cp.start()
        pending.append(cp)
        return cp

    def got(group):
        for cp in group:
            cp.wait_recv()

    load_q = pltpu.make_async_copy(queue, Q, lsem.at[0])
    load_q.start()

    refreshed = RATE * wk_in[...] + (1.0 - RATE) * wq_in[...]
    ref_o[...] = refreshed
    low = jnp.where(c == 0, refreshed[:, :HALF], refreshed[:, HALF:])
    tail = jnp.concatenate([low[16:24], jnp.zeros((8, HALF), F32)], axis=0)
    GA[y, z] = q_in[0:16]
    GB[y, z] = q_in[16:32]
    GP[y, z] = pool_in[...]
    GW[y, z] = jnp.concatenate([low[0:16], tail], axis=1).astype(BF16)
    POSY[y] = jnp.zeros((8, 128), jnp.int32)
    POSY[y, 0:1, 0:32] = pos_in[...]

    barrier = pltpu.get_barrier_semaphore()
    peers = [zdev(d) for d in range(1, NZ)] + [ydev(d) for d in range(1, NY)]
    peers += [xdev(1), xdev(3), core]
    for dev in peers:
        pl.semaphore_signal(barrier, inc=1, device_id=dev, device_id_type=MESH)
    pl.semaphore_wait(barrier, len(peers))

    class YFirst:
        def __init__(self, ref):
            self.ref, self.s = ref, 0
            self.cps = [start(ref.at[y, z], ref.at[y, z], ydev(d)) for d in (1, 3, 2)]

        def step(self):
            got(self.cps)
            ref, s = self.ref, self.s + 1
            self.s = s
            r, l = zi(1 - s), zi(s - 1)
            if s < 4:
                self.cps = [start(ref.at[:, r], ref.at[:, r], zdev(1)),
                            start(ref.at[:, l], ref.at[:, l], zdev(-1))]
            else:
                self.cps = [start(ref.at[:, r, :, :HALF], ref.at[:, r, :, :HALF], zdev(1)),
                            start(ref.at[:, l, :, HALF:], ref.at[:, l, :, HALF:], zdev(-1))]

        def end(self):
            got(self.cps)

    class ZFirst:
        def __init__(self, ref):
            self.ref, self.s, self.cps = ref, 0, []
            self.step()

        def step(self):
            got(self.cps)
            ref, s = self.ref, self.s + 1
            self.s = s
            r, l = zi(1 - s), zi(s - 1)
            if s < 4:
                self.cps = [start(ref.at[y, r], ref.at[y, r], zdev(1)),
                            start(ref.at[y, l], ref.at[y, l], zdev(-1))]
            elif s == 4:
                self.cps = [start(ref.at[y, r, :, :HALF], ref.at[y, r, :, :HALF], zdev(1)),
                            start(ref.at[y, l, :, HALF:], ref.at[y, l, :, HALF:], zdev(-1))]
            elif s == 5:
                self.cps = [start(ref.at[y], ref.at[y], ydev(1)), start(ref.at[y], ref.at[y], ydev(-1))]
            else:
                u, d = yi(-1), yi(1)
                self.cps = [start(ref.at[u, :, :, :HALF], ref.at[u, :, :, :HALF], ydev(1)),
                            start(ref.at[d, :, :, HALF:], ref.at[d, :, :, HALF:], ydev(-1))]

        def end(self):
            got(self.cps)

    left, right, far = (((x + d) % 4) * 2 + c for d in (3, 1, 2))
    pieces, passed, cs = [], [], []

    def along_x(*offsets):
        for d in offsets:
            src, dst = GP.at[:, zi(d)], PALL.at[b, :, zi(d)]
            pieces.append((d, start(src, dst, xdev(1)), start(src, dst, xdev(-1))))

    def pass_x(n):
        for _ in range(n):
            d, up, down = pieces.pop(0)
            up.wait_recv()
            down.wait_recv()
            l, r = PALL.at[left, :, zi(d), :, :HALF], PALL.at[right, :, zi(d), :, HALF:]
            passed.append(start(l, l, xdev(1)))
            passed.append(start(r, r, xdev(-1)))

    pos_y = [start(POSY.at[y], POSY.at[y], ydev(d)) for d in (1, 2, 3)]
    ga = YFirst(GA)
    gb = ZFirst(GB)
    gp = YFirst(GP)
    got(pos_y)
    POSC[...] = jnp.zeros((8, 128), jnp.int32)
    for d in range(NY):
        POSC[d:d + 1] = POSY[d, 0:1]
    POSZ[z] = POSC[...]
    pos_z = [start(POSC, POSZ.at[z], zdev(d)) for d in range(1, NZ)]
    ga.step()
    gb.step()
    got(pos_z)
    load_q.wait()

    post = POSZ[...].reshape(64, 128).astype(F32).T - (k * KEYS).astype(F32)

    def positives(p, mid):
        col = jnp.concatenate([post[0:32, 8 * j + p:8 * j + p + 1] for j in range(8)], axis=0)
        for t in range(KEYS // TILE):
            if t == 4:
                for f in mid:
                    f()
            at = lax.broadcasted_iota(jnp.int32, (ROWS, TILE), 1) + t * TILE
            hot = jnp.where(at.astype(F32) == col, 1.0, 0.0).astype(BF16)
            d = jnp.dot(hot, Q[t * TILE:(t + 1) * TILE, :], preferred_element_type=F32)
            if t == 0:
                ACC[...] = d
            else:
                ACC[...] += d
        QP[p] = ACC[...].reshape(8, 32, D).astype(BF16)

    positives(0, [ga.step, gb.step])
    positives(1, [gb.step])
    ga.step()
    positives(2, [gb.step])
    positives(3, [ga.step])

    lane = lax.broadcasted_iota(jnp.int32, (ROWS, 128), 1)

    def scores(parts, mid):
        X = jnp.concatenate([p() for p in parts], axis=0)
        mx = jnp.full((ROWS, 128), -3e38, F32)
        for t in range(KEYS // TILE):
            if t == 4:
                for f in mid:
                    f()
            s = lax.dot_general(X, Q[t * TILE:(t + 1) * TILE, :], (((1,), (1,)), ((), ())),
                                preferred_element_type=F32)
            S[:, t * TILE:(t + 1) * TILE] = s
            for j in range(TILE // 128):
                mx = jnp.maximum(mx, s[:, j * 128:(j + 1) * 128])
        XC[...] = X
        return jnp.max(mx, axis=1, keepdims=True)

    def partial(m, positive_rows, mid):
        total = jnp.zeros((ROWS, 128), F32)
        for t in range(KEYS // TILE):
            if t == 4:
                for f in mid:
                    f()
            e = jnp.exp2((S[:, t * TILE:(t + 1) * TILE] - m) * EXP2)
            for j in range(TILE // 128):
                total = total + e[:, j * 128:(j + 1) * 128]
            d = jnp.dot(e.astype(BF16), Q[t * TILE:(t + 1) * TILE, :], preferred_element_type=F32)
            if t == 0:
                ACC[...] = d
            else:
                ACC[...] += d
        l = jnp.sum(total, axis=1, keepdims=True)
        R = jnp.concatenate([p() for p in positive_rows], axis=0)
        ps = jnp.sum(XC[...].astype(F32) * R.astype(F32), axis=1, keepdims=True)
        return jnp.where(lane == 0, m, jnp.where(lane == 1, l, ps)).T

    def scores_a(zs, mid):
        return scores([lambda d=d: GA[:, zi(d)].reshape(64, D) for d in zs], mid)

    def partial_a(m, zs, mid):
        stats = partial(m, [lambda d=d: QP[:, zi(d), 0:16].reshape(64, D) for d in zs], mid)
        for n, d in enumerate(zs):
            OA[:, zi(d)] = ACC[n * 64:(n + 1) * 64].reshape(NY, 16, D)
            for r in range(3):
                SA[pl.ds(r * NZ + zi(d), 1), 0:64] = stats[r:r + 1, n * 64:(n + 1) * 64]

    def scores_b(ys, mid):
        return scores([lambda d=d: GB[yi(d)].reshape(128, D) for d in ys], mid)

    def partial_b(m, ys, mid):
        stats = partial(m, [lambda d=d: QP[yi(d), :, 16:32].reshape(128, D) for d in ys], mid)
        for n, d in enumerate(ys):
            OB[yi(d)] = ACC[n * 128:(n + 1) * 128].reshape(NZ, 16, D)
            for r in range(3):
                SB[pl.ds(r * NY + yi(d), 1), :] = stats[r:r + 1, n * 128:(n + 1) * 128]

    SA[...] = jnp.zeros_like(SA)
    SB[...] = jnp.zeros_like(SB)
    first_a, second_a = (0, 1, -1, 2), (-2, 3, -3, 4)

    def pool_step(n):
        gp.step()
        if n == 0:
            along_x(0)
        else:
            along_x(n, -n)

    gw = ZFirst(GW)
    m = scores_a(first_a, [lambda: pool_step(0)])
    gb.step()
    gw.step()
    partial_a(m, first_a, [lambda: pool_step(1)])
    ga.end()
    pass_x(1)
    gw.step()
    m = scores_a(second_a, [lambda: pool_step(2)])
    gw.step()
    partial_a(m, second_a, [lambda: pool_step(3)])

    def combine(ref, n, h):
        parts = [ref[i] for i in range(n)]
        top = functools.reduce(jnp.maximum, [p[0:h] for p in parts])
        total = sum(p[h:2 * h] * jnp.exp2((p[0:h] - top) * EXP2) for p in parts)
        positive = sum(p[2 * h:3 * h] for p in parts)
        return top, total, positive

    class Stats:
        def __init__(self, own, ys, mid, zs, h):
            self.own, self.ys, self.mid, self.zs, self.h = own, ys, mid, zs, h
            ys[y] = own[...]
            self.cps = [start(own, ys.at[y], ydev(d)) for d in (1, 2, 3)]

        def step(self):
            got(self.cps)
            h, mid, zs = self.h, self.mid, self.zs
            top, total, positive = combine(self.ys, NY, h)
            mid[0:h], mid[h:2 * h], mid[2 * h:3 * h] = top, total, positive
            zs[z] = mid[...]
            self.cps = [start(mid, zs.at[z], zdev(d)) for d in range(1, NZ)]

        def end(self, row, at):
            got(self.cps)
            h = self.h
            top, total, positive = combine(self.zs, NZ, h)
            w = jnp.exp2((self.own[0:h] - top) * EXP2) / total
            LS[0:h] = jnp.log(total) + (top - positive) * SIM
            for i in range(h):
                WC[i] = jnp.broadcast_to(w[i:i + 1], (128, 128)).T
            return pltpu.roll(jnp.broadcast_to(LS[pl.ds(row, 1), :], (8, 128)), at % 128, 1)[0:1]

    def scale_a(i, carry):
        w = WC[i, 0:64].reshape(NY, 16, 128)
        for j in range(D // 128):
            n = slice(j * 128, (j + 1) * 128)
            OA[:, i, :, n] = OA[:, i, :, n] * w - QP[:, i, 0:16, n].astype(F32)
        return carry

    def scale_b(i, carry):
        w = WC[i].reshape(NZ, 16, 128)
        for j in range(D // 128):
            n = slice(j * 128, (j + 1) * 128)
            OB[i, :, :, n] = OB[i, :, :, n] * w - QP[i, :, 16:32, n].astype(F32)
        return carry

    class Ring:
        def __init__(self, n, me, dev, get, sr, sl, rr, rl):
            self.n, self.h, self.me, self.dev, self.get = n, n // 2, me, dev, get
            self.sr, self.sl, self.rr, self.rl = sr, sl, rr, rl
            self.s, self.pair = 0, None

        def step(self):
            n, h = self.n, self.h
            self.s += 1
            s = self.s
            dr, dl = (self.me + h + 1 - s) % n, (self.me + n - h - 1 + s) % n
            sr, sl, rr, rl = (r.at[s - 1] for r in (self.sr, self.sl, self.rr, self.rl))
            if s == 1:
                sr[..., :HALF] = self.get(dr)[..., :HALF]
                sl[..., HALF:] = self.get(dl)[..., HALF:]
                sr, rr = (r.at[..., :HALF] for r in (sr, rr))
                sl, rl = (r.at[..., HALF:] for r in (sl, rl))
            else:
                got(self.pair)
                pr, plf = self.rr.at[s - 2], self.rl.at[s - 2]
                if s == 2:
                    sr[..., :HALF] = self.get(dr)[..., :HALF] + pr[..., :HALF]
                    sr[..., HALF:] = self.get(dr)[..., HALF:]
                    sl[..., :HALF] = self.get(dl)[..., :HALF]
                    sl[..., HALF:] = self.get(dl)[..., HALF:] + plf[..., HALF:]
                else:
                    sr[...] = self.get(dr) + pr[...]
                    sl[...] = self.get(dl) + plf[...]
            self.pair = (start(sr, rr, self.dev(1)), start(sl, rl, self.dev(-1)))

        def end(self):
            got(self.pair)
            return self.get(self.me) + self.rr[self.h - 1] + self.rl[self.h - 1]

    first_b, second_b = (0, 1), (-1, 2)
    ta = Stats(SA, SAY, SAC, SAZ, NZ)

    gb.end()
    gw.step()
    gp.end()
    along_x(4)
    cs.append(start(GP, PALL.at[b], core))
    m = scores_b(first_b, [ta.step])
    pass_x(2)
    partial_b(m, first_b, [])
    ra = Ring(NZ, z, zdev, lambda d: OA[:, d], SAR, SAL, RAR, RAL)
    loss_o[0:1, 0:16] = ta.end(z, 128 - y * 16)[:, 0:16]
    lax.fori_loop(0, NZ, scale_a, 0)
    ra.step()
    gw.step()
    pass_x(2)
    m = scores_b(second_b, [])
    ra.step()
    pass_x(2)
    partial_b(m, second_b, [])
    tb = Stats(SB, SBY, SBC, SBZ, NY)
    gw.end()
    wcopy = start(GW, WH.at[c], core)
    pass_x(1)
    tb.step()

    wcopy.wait_recv()

    def unpack(i, carry):
        own = GW[i // NZ, i % NZ].astype(F32)
        other = WH[1 - c, i // NZ, i % NZ].astype(F32)
        at = pl.multiple_of(i * 24, 8)
        for h in range(2):
            part = jnp.where(c == h, own, other)
            n = slice(h * HALF, (h + 1) * HALF)
            WF[pl.ds(at, 16), n] = part[:, :HALF]
            WF[pl.ds(at + 16, 8), n] = part[0:8, HALF:]
        return carry

    lax.fori_loop(0, NY * NZ, unpack, 0)
    WB[...] = WF[...].astype(BF16)
    ra.step()
    loss_o[0:1, 16:32] = tb.end(y, 144 - z * 16)[:, 16:32]
    lax.fori_loop(0, NY, scale_b, 0)
    rb = Ring(NY, y, ydev, lambda d: OB[d], SBR, SBL, RBR, RBL)
    rb.step()
    own_pool = pltpu.make_async_copy(GP, PALL.at[b], lsem.at[1])
    own_pool.start()
    got(passed)
    cs.extend(start(PALL.at[p], PALL.at[p], core) for p in (left, right, far))
    ra.step()
    rb.step()
    own_pool.wait()
    got(cs)

    def keys(i, carry):
        for p in range(NY):
            KV[i, p * 128:(p + 1) * 128, :] = jnp.dot(
                PALL[i, p].reshape(128, D), WB[...], preferred_element_type=F32).astype(BF16)
        return carry

    lax.fori_loop(0, 6, keys, 0)
    TA[...] = ra.end()
    YA[y] = TA[y]
    ya = [start(TA.at[yi(d)], YA.at[y], ydev(d)) for d in (1, 2, 3)]
    lax.fori_loop(6, 8, keys, 0)
    out_keys = pltpu.make_async_copy(KV, keys_o, lsem.at[1])
    out_keys.start()
    got(ya)
    grad_o[0:16] = (YA[0] + YA[1] + YA[2] + YA[3]) * SIM
    TB[...] = rb.end()
    rc = Ring(NZ, z, zdev, lambda d: TB[d], SCR, SCL, RCR, RCL)
    rc.step()
    rc.step()
    rc.step()
    rc.step()
    grad_o[16:32] = rc.end() * SIM
    for cp in pending:
        cp.wait_send()
    out_keys.wait()


def any_spec():
    return pl.BlockSpec(memory_space=pl.ANY)


def vmem_spec():
    return pl.BlockSpec(memory_space=pltpu.VMEM)


NSEM = 160


def run_main(queries, pooled, pos, wq, wk, queue):
    z4, y2 = (4, NY, 16, D), (2, NZ, 16, D)
    grid = (NY, NZ, 16, D)
    scratch = [pltpu.VMEM((KEYS, D), BF16)] + [pltpu.VMEM(grid, BF16)] * 4
    scratch += [
        pltpu.VMEM((NY, 8, 128), jnp.int32), pltpu.VMEM((8, 128), jnp.int32), pltpu.VMEM((NZ, 8, 128), jnp.int32),
        pltpu.VMEM((ROWS, D), BF16), pltpu.VMEM((ROWS, KEYS), F32),
        pltpu.VMEM((ROWS, D), F32), pltpu.VMEM(grid, F32), pltpu.VMEM(grid, F32),
        pltpu.VMEM((NY, NZ, 32, D), BF16), pltpu.VMEM((2,) + grid, BF16), pltpu.VMEM((D, D), F32),
        pltpu.VMEM((D, D), BF16), pltpu.VMEM((8, 512, D), BF16), pltpu.VMEM((8,) + grid, BF16),
        pltpu.VMEM((24, 128), F32), pltpu.VMEM((NY, 24, 128), F32), pltpu.VMEM((24, 128), F32),
        pltpu.VMEM((NZ, 24, 128), F32), pltpu.VMEM((16, 128), F32), pltpu.VMEM((NY, 16, 128), F32),
        pltpu.VMEM((16, 128), F32), pltpu.VMEM((NZ, 16, 128), F32),
        pltpu.VMEM((8, 128), F32), pltpu.VMEM((8, 128, 128), F32),
    ]
    scratch += [pltpu.VMEM(z4, F32)] * 4 + [pltpu.VMEM(y2, F32)] * 4
    scratch += [pltpu.VMEM((NY, 16, D), F32)] * 2 + [pltpu.VMEM((NZ, 16, D), F32)]
    scratch += [pltpu.VMEM((4, 16, D), F32)] * 4
    scratch += [pltpu.SemaphoreType.DMA((NSEM,)), pltpu.SemaphoreType.DMA((NSEM,)), pltpu.SemaphoreType.DMA((2,))]
    return pl.pallas_call(
        main_kernel,
        name="retrieval",
        out_shape=[
            jax.ShapeDtypeStruct((1, 32), F32), jax.ShapeDtypeStruct((32, D), F32),
            jax.ShapeDtypeStruct((24, D), F32), jax.ShapeDtypeStruct((8, 512, D), BF16),
        ],
        in_specs=[vmem_spec()] * 5 + [any_spec()],
        out_specs=[vmem_spec()] * 3 + [any_spec()],
        scratch_shapes=scratch,
        compiler_params=pltpu.CompilerParams(
            collective_id=0, has_side_effects=True, vmem_limit_bytes=60 * 2**20),
        cost_estimate=pl.CostEstimate(flops=20 * 10**9, bytes_accessed=32 * 10**6, transcendentals=4 * 10**6),
    )(queries, pooled, pos, wq, wk, queue)


BLK = 512
WIN = BLK + 16


def enqueue_kernel(shift_ref, queue, keys, nq, BUF, WV, isem, osem, ksem):
    shift = shift_ref[0]
    steps = KEYS // BLK

    def block(i):
        rows = pl.ds(i * BLK, BLK)
        at = i * BLK + shift
        base = pl.multiple_of(jnp.clip(at // 16 * 16, 0, KEYS - WIN), 16)
        return (at, base, (at > -BLK) & (at < KEYS),
                pltpu.make_async_copy(queue.at[rows, :], BUF.at[i], isem.at[i]),
                pltpu.make_async_copy(BUF.at[i], nq.at[rows, :], osem.at[i]),
                pltpu.make_async_copy(keys.at[pl.ds(base, WIN), :], WV.at[i], ksem.at[i]))

    for i in range(steps):
        _, _, lands, load, _, fetch = block(i)
        load.start()

        @pl.when(lands)
        def _():
            fetch.start()

    for i in range(steps):
        at, base, lands, load, store, fetch = block(i)
        load.wait()

        @pl.when(lands)
        def _():
            fetch.wait()
            new = pltpu.roll(WV[i].astype(F32), (2 * WIN + base - at) % WIN, 0)[:BLK]
            row = lax.broadcasted_iota(jnp.int32, (BLK, 1), 0) + at
            ok = (row >= 0) & (row < KEYS)
            BUF[i] = jnp.where(ok, new, BUF[i].astype(F32)).astype(BF16)

        store.start()
    for i in range(steps):
        block(i)[4].wait()


def run_enqueue(shift, queue, keys):
    steps = KEYS // BLK
    return pl.pallas_call(
        enqueue_kernel,
        name="enqueue",
        out_shape=jax.ShapeDtypeStruct((KEYS, D), BF16),
        in_specs=[pl.BlockSpec(memory_space=pltpu.SMEM)] + [any_spec()] * 2,
        out_specs=any_spec(),
        scratch_shapes=[pltpu.VMEM((steps, BLK, D), BF16), pltpu.VMEM((steps, WIN, D), BF16)]
        + [pltpu.SemaphoreType.DMA((steps,))] * 3,
        compiler_params=pltpu.CompilerParams(vmem_limit_bytes=60 * 2**20),
    )(shift, queue, keys)


def local(queries, positives, queue, pointer, pooled, query_projection_weight, key_weight):
    loss, grad, refreshed, keys = run_main(
        queries, pooled, positives.reshape(1, 32), query_projection_weight, key_weight, queue)
    first_row = lax.axis_index("queue") * KEYS
    shift = (first_row - pointer + KEYS * NY * NZ) % (KEYS * NY * NZ)
    shift = jnp.where(shift >= KEYS, shift - KEYS * NY * NZ, shift)
    new_queue = run_enqueue(shift, queue, keys.reshape(KEYS, D))
    return loss.reshape(32), grad, new_queue, refreshed


def solution(mesh):
    both = P(("batch", "queue"), None)
    one = P("queue", None)
    return jax.shard_map(
        local,
        mesh=mesh,
        in_specs=(both, P(("batch", "queue")), one, P(), both, one, one),
        out_specs=(P(("batch", "queue")), both, one, one),
        check_vma=False,
    )
```

time: 250 us -> 118 us (0.47)
  the two profiles are of different devices: /device:TPU:47 before, /device:TPU:6 now
where the time goes in v2:
time: 118 us
  Pallas kernels  115 us (97%)
  local copies, waits for them, and re-layouts  1.8 us (2%)
  between operations  1.35 us (1%)
    pallas_call x1, Pallas kernels, run_main(): pl.pallas_call(main_kernel, name='retrieval', out_shape=[jax.ShapeDtypeSt...  110 us
    pallas_call x1, Pallas kernels, run_enqueue(): pl.pallas_call(enqueue_kernel, name='enqueue', out_shape=jax.ShapeDtypeSt...  5.64 us

profile of v2, /device:TPU:6, one launch (start us, length us, event | category | flops | bytes accessed | tf_op | source)
XLA Modules:
  0.0 118.3 jit_solution(2147878670643060247)
XLA Ops:
  1.3 109.5 %retrieval.1 = (f32[1,32]{1,0:T(1,128)}, f32[32,768]{1,0:T(8,128)}, f32[24,768]{1,0:T(8,128)}, bf16[8,512,768]{2,1,0:T(8,128)(2,1)}) custom-call(bf16[32,768]{1,0:T(8,128)(2,1)} %q_in.1, bf16[16,768]{1,0:T(8,128)(2,1)} %pool_in.1, s32[1,32]{1,0:T(1,128)} %bitcast.5, f32[24,768]{1,0:T(8,128)} %wq_in.1, f32[24,768]{1,0:T(8,128)} %wk_in.1, bf16[4096,768]{1,0:T(8,128)(2,1)} %queue.3), custom_call_target="tpu_custom_call" | custom-call | flops 20000000000 | bytes 32000000 | tf_op jit(solution)/shard_map/retrieval/pallas_call | solution.py:463
  110.8 0.0 copy-start.2
  110.8 0.0 copy-start
  110.8 0.0 copy-start.1
  110.9 5.6 %enqueue.1 = bf16[4096,768]{1,0:T(8,128)(2,1)} custom-call(s32[1]{0:T(128)S(6)} %select_n.12.shift_ref, bf16[4096,768]{1,0:T(8,128)(2,1)} %queue.3, bf16[4096,768]{1,0:T(8,128)(2,1)} %bitcast.4), custom_call_target="tpu_custom_call" | custom-call | tf_op jit(solution)/shard_map/enqueue/pallas_call | solution.py:523
  116.5 0.0 copy-done.2
  116.5 0.5 copy.15
  117.0 0.0 copy-done
  117.0 0.6 copy.16
  117.7 0.0 copy-done.1
  117.7 0.6 copy.17
Async XLA Ops:
  110.8 5.7 %copy-start.2 = (f32[1,32]{1,0:T(1,128)S(1)}, f32[1,32]{1,0:T(1,128)}, u32[]{:S(2)}) copy-start(f32[1,32]{1,0:T(1,128)} %get-tuple-element.8) | copy-start | bytes 388
  110.8 6.2 %copy-start = (f32[32,768]{1,0:T(8,128)S(1)}, f32[32,768]{1,0:T(8,128)}, u32[]{:S(2)}) copy-start(f32[32,768]{1,0:T(8,128)} %get-tuple-element.17) | copy-start | bytes 294916
  110.8 6.8 %copy-start.1 = (f32[24,768]{1,0:T(8,128)S(1)}, f32[24,768]{1,0:T(8,128)}, u32[]{:S(2)}) copy-start(f32[24,768]{1,0:T(8,128)} %get-tuple-element.19) | copy-start | bytes 221188
